TPU v7x, 256 devices: a whole 4x4x8 slice. The times are simulated.
256 devices in a mesh: dp: 8 (over z), seq: 32 (over y, x, core).
Axes of the slice: x: 4, y: 4, z: 8, core: 2. Of those that a mesh axis runs over, the one named last changes fastest.
Arguments:
- query: bfloat16 [8, 4096, 4096], P('dp', 'seq'), may hold values from -1.796875 to 1.796875
- key_in: bfloat16 [8, 4096, 4096], P('dp', 'seq'), may hold values from -1.796875 to 1.796875
- value_in: bfloat16 [8, 4096, 4096], P('dp', 'seq'), may hold values from -17 to 17
- cotangent: bfloat16 [8, 4096, 4096], P('dp', 'seq'), may hold values from -6 to 6
- gain: float32 [4096], replicated, may hold values from 0.1 to 1.9
Outputs:
- grad_query: bfloat16 [8, 4096, 4096], P('dp', 'seq')
- grad_key: bfloat16 [8, 4096, 4096], P('dp', 'seq')
- grad_value: bfloat16 [8, 4096, 4096], P('dp', 'seq')
- grad_gain: float32 [4096], replicated
All inputs are finite; a program needn't handle non-finite values.
Results may differ from a plain program's by a relative error of at most 0.011.
Values sent between devices are 32-bit elements; how exact they have to be, the bound alone decides.
A program may use at most 320 MiB of HBM per device.

v0:
```python
import math

import jax
import jax.numpy as jnp
from jax import lax
from jax.sharding import PartitionSpec as P

HD = 128


def carried_in(value, axis, join, neutral, backward):
    count, mine = (lax.axis_size(axis), lax.axis_index(axis))
    pieces = lax.all_gather(value, axis)
    if backward:
        pieces = pieces[::-1]
        mine = count - 1 - mine
    running = jnp.full_like(value, 0) + jnp.asarray(neutral, value.dtype)

    def step(position, running):
        longer = join(running, pieces[position])
        return jnp.where(position < mine, longer, running)

    return lax.fori_loop(0, count - 1, step, running)


def add_states(earlier, later):
    return earlier + later


def split_state(state):
    upper = state.astype(jnp.bfloat16)
    lower = (state - upper.astype(jnp.float32)).astype(jnp.bfloat16)
    return (upper, lower)


def state_product(form, data, parts):
    upper, lower = parts
    first = jnp.einsum(form, data, upper, preferred_element_type=jnp.float32)
    return first + jnp.einsum(form, data, lower, preferred_element_type=jnp.float32)


def shards(query, key_in, value_in, cotangent, gain):
    tok_rows = query.shape[1]
    width = query.shape[2]
    heads = width // HD
    q_blk = query[0].reshape(tok_rows, heads, HD)
    k_blk = key_in[0].reshape(tok_rows, heads, HD)
    v_blk = value_in[0].reshape(tok_rows, heads, HD)
    dy_f = cotangent[0].astype(jnp.float32)
    positions = jnp.arange(tok_rows)
    causal = (positions[:, None] >= positions[None, :])[None]
    zeros = jnp.zeros((heads, HD, HD), jnp.float32)
    own_state = jnp.einsum("thd,the->hde", k_blk, v_blk, preferred_element_type=jnp.float32)
    prefix = carried_in(own_state, "seq", add_states, zeros, False)
    prefix_parts = split_state(prefix)
    scores = jnp.einsum("thd,shd->hts", q_blk, k_blk, preferred_element_type=jnp.float32)
    masked = jnp.where(causal, scores, 0.0).astype(jnp.bfloat16)
    attn = jnp.einsum("hts,she->the", masked, v_blk, preferred_element_type=jnp.float32)
    attn = attn + state_product("thd,hde->the", q_blk, prefix_parts)
    flat = attn.reshape(tok_rows, width)
    scale = lax.rsqrt(jnp.mean(flat * flat, axis=-1, keepdims=True) + 1e-06)
    normed = flat * scale
    gain_sum = lax.psum(jnp.sum(dy_f * normed, axis=0), ("dp", "seq"))
    total_rows = tok_rows * lax.axis_size("dp") * lax.axis_size("seq")
    grad_gain = gain_sum / math.sqrt(total_rows)
    dnorm = dy_f * gain
    inner = jnp.mean(dnorm * normed, axis=-1, keepdims=True)
    grad_attn = (scale * (dnorm - normed * inner)).astype(jnp.bfloat16).reshape(tok_rows, heads, HD)
    gstate = jnp.einsum("thd,the->hde", q_blk, grad_attn, preferred_element_type=jnp.float32)
    suffix = carried_in(gstate, "seq", add_states, zeros, True)
    suffix_parts = split_state(suffix)
    dscore = jnp.einsum("the,she->hts", grad_attn, v_blk, preferred_element_type=jnp.float32)
    dmask = jnp.where(causal, dscore, 0.0).astype(jnp.bfloat16)
    grad_q = jnp.einsum("hts,shd->thd", dmask, k_blk, preferred_element_type=jnp.float32)
    grad_q = grad_q + state_product("the,hde->thd", grad_attn, prefix_parts)
    grad_k = jnp.einsum("hts,thd->shd", dmask, q_blk, preferred_element_type=jnp.float32)
    grad_k = grad_k + state_product("she,hde->shd", v_blk, suffix_parts)
    grad_v = jnp.einsum("hts,the->she", masked, grad_attn, preferred_element_type=jnp.float32)
    grad_v = grad_v + state_product("shd,hde->she", k_blk, suffix_parts)
    out_shape = (1, tok_rows, width)
    return (
        grad_q.astype(jnp.bfloat16).reshape(out_shape),
        grad_k.astype(jnp.bfloat16).reshape(out_shape),
        grad_v.astype(jnp.bfloat16).reshape(out_shape),
        grad_gain,
    )


def solution(mesh):
    placed = (
        P("dp", "seq", None),
        P("dp", "seq", None),
        P("dp", "seq", None),
        P("dp", "seq", None),
        P(),
    )
    return jax.shard_map(
        shards,
        mesh=mesh,
        in_specs=placed,
        out_specs=(P("dp", "seq", None), P("dp", "seq", None), P("dp", "seq", None), P()),
        check_vma=False,
    )
```

profile of v0, /device:TPU:1, one launch (start us, length us, event | category | flops | bytes accessed | tf_op | source)
XLA Modules:
  0.0 655.2 jit_solution(11479863262526753310)
XLA Ops:
  12.3 2.4 copy.72
  14.7 2.6 copy.46
  17.3 2.5 select_convert_fusion.1
  23.0 199.7 %all-gather.5.cloned.1.call-done = f32[1024,128,128]{2,1,0:T(8,128)} async-done(((f32[32,128,128]{2,1,0:T(8,128)}), f32[1024,128,128]{2,1,0:T(8,128)}) %all-gather.5.cloned.1.call-update) | async-done | bytes 67108880 | tf_op jit(solution)/shard_map/all_gather | solution.py:13
  222.6 72.4 %while.28 = (s32[]{:T(128)}, f32[32,128,128]{2,1,0:T(8,128)S(1)}, s32[]{:T(128)}, f32[32,32,128,128]{3,2,1,0:T(8,128)}, s32[]{:T(128)}, /*index=5*/s32[]{:T(128)}) while((s32[]{:T(128)}, f32[32,128,128]{2,1,0:T(8,128)S(1)}, s32[]{:T(128)}, f32[32,32,128,128]{3,2,1,0:T(8,128)}, s32[]{:T(128)}, /*index=5*/s32[]{:T(128)}) %tuple.67), condition=%wide.region_1.2_spmd.clone, body=%wide.region_0.1_spmd.clone.sunk | while | flops 1572868 | bytes 6291549 | solution.py:23
  225.0 2.3 add_select_fusion.4
  227.3 2.3 add_select_fusion.4
  229.7 2.3 add_select_fusion.4
  232.0 2.3 add_select_fusion.4
  234.3 2.3 add_select_fusion.4
  236.7 2.3 add_select_fusion.4
  239.0 2.3 add_select_fusion.4
  241.3 2.3 add_select_fusion.4
  243.7 2.3 add_select_fusion.4
  246.0 2.3 add_select_fusion.4
  248.3 2.3 add_select_fusion.4
  250.7 2.3 add_select_fusion.4
  253.0 2.3 add_select_fusion.4
  257.7 2.3 add_select_fusion.4
  260.0 2.3 add_select_fusion.4
  262.4 2.3 add_select_fusion.4
  295.1 2.9 fusion.20
  298.0 2.4 multiply_reduce_fusion
  300.5 3.1 copy.47
  303.5 2.8 fusion.4
  319.4 77.8 %psum.7 = f32[4096]{0:T(1024)S(1)} all-reduce(f32[4096]{0:T(1024)S(1)} %get-tuple-element.202), channel_id=1, replica_groups=mesh['dp'=8,'seq'=32] {'dp','seq'}, use_global_device_ids=true, to_apply=%region_7.8 | all-reduce | flops 4096 | bytes 32768 | tf_op jit(solution)/shard_map/psum | solution.py:63
  397.8 3.3 fusion.30
  401.2 116.0 %all-gather.7.cloned.1.call-done = f32[1024,128,128]{2,1,0:T(8,128)} async-done(((f32[32,128,128]{2,1,0:T(8,128)}), f32[1024,128,128]{2,1,0:T(8,128)}) %all-gather.7.cloned.1.call-update) | async-done | bytes 67108880 | tf_op jit(solution)/shard_map/all_gather | solution.py:13
  517.1 43.8 %rev.3 = f32[32,32,128,128]{3,2,1,0:T(8,128)} reverse(f32[32,32,128,128]{3,2,1,0:T(8,128)} %bitcast.12), dimensions={0} | reverse | bytes 134217728 | tf_op jit(solution)/shard_map/rev | solution.py:15
  560.9 72.4 %while.29 = (s32[]{:T(128)}, f32[32,128,128]{2,1,0:T(8,128)S(1)}, s32[]{:T(128)}, f32[32,32,128,128]{3,2,1,0:T(8,128)}, s32[]{:T(128)}, /*index=5*/s32[]{:T(128)}) while((s32[]{:T(128)}, f32[32,128,128]{2,1,0:T(8,128)S(1)}, s32[]{:T(128)}, f32[32,32,128,128]{3,2,1,0:T(8,128)}, s32[]{:T(128)}, /*index=5*/s32[]{:T(128)}) %tuple.70), condition=%wide.region_5.6_spmd.clone, body=%wide.region_4.5_spmd.clone.sunk | while | flops 1572868 | bytes 6291549 | solution.py:23
  641.7 2.4 copy.64
  644.1 2.9 fusion
  (114 shorter events, 137.9 us)
Async XLA Ops:
  7.2 215.5 %all-gather.5.cloned.1.call-start = ((), (), s32[]{:S(2)}) async-start(), calls=%async_computation | async-start | bytes 69206016 | tf_op jit(solution)/shard_map/all_gather | solution.py:13
  7.2 2.6 copy-start.18
  8.8 1.0 copy-start.8
  9.8 2.4 copy-start.10
  12.2 504.9 %all-gather.7.cloned.1.call-start = ((), (), s32[]{:S(2)}) async-start(), calls=%async_computation.1 | async-start | bytes 69206016 | tf_op jit(solution)/shard_map/all_gather | solution.py:13
  19.8 1.0 copy-start.17
  295.1 2.9 copy-start
  295.1 2.9 copy-start.2
  295.1 3.0 copy-start.12
  300.5 3.1 copy-start.19
  300.5 5.8 copy-start.13
  303.5 2.8 copy-start.7
  306.3 1.8 copy-start.3
  307.1 1.0 copy-start.5
  310.7 2.2 copy-start.11
  313.0 1.0 copy-start.15
  313.0 2.0 copy-start.1
  313.0 2.2 copy-start.6
  637.6 2.2 copy-start.9
  637.6 2.2 copy-start.14
  641.7 2.4 copy-start.4
  641.7 2.4 copy-start.16
Sparse Core Ops, SparseCore 0:
  12.3 210.2 all-gather.4
  310.8 206.2 all-gather.6
where the time goes:
time: 658 us; the launch traced here: 655 us
  waiting for transfers between devices  316 us (48%)
  other arithmetic  147 us (22%)
  blocking collectives  77.8 us (12%)
  local copies, waits for them, and re-layouts  66 us (10%)
  matrix products  32.5 us (5%)
  between operations  14.3 us (2%)
    all_gather x2, waiting for transfers between devices, carried_in(): pieces = lax.all_gather(value, axis)  316 us
    select_n x62, other arithmetic, step(): return jnp.where(position < mine, longer, running)  143 us
    psum x1, blocking collectives, shards(): gain_sum = lax.psum(jnp.sum(dy_f * normed, axis=0), ('dp', 'seq'))  77.8 us
    rev x1, local copies, waits for them, and re-layouts, carried_in(): pieces = pieces[::-1]  43.8 us
    unnamed x46, local copies, waits for them, and re-layouts  13.6 us
  transfers between devices with their start and end apart: 2, of which 2 were waited for; matrix products, arithmetic and copies ran while one was open for 3% of the time, Pallas kernels for 0%

commit v1 on v0

v1 whole, which is shorter than its diff:
```python
import functools
import math

import jax
import jax.numpy as jnp
from jax import lax
from jax.experimental import pallas as pl
from jax.experimental.pallas import tpu as pltpu
from jax.sharding import PartitionSpec as P

HD = 128
TOK = 128
HEADS = 32
F = HEADS * HD
HALF = HEADS // 2
SIDE = 4
CHIPS = SIDE * SIDE
DP = 8
G = 2
HG = HALF // G
MESH = pl.DeviceIdType.MESH
F32 = jnp.float32
BF16 = jnp.bfloat16

OFFSETS = [(dy, dx) for dy in range(SIDE) for dx in range(SIDE) if (dy, dx) != (0, 0)]
N_OFF = len(OFFSETS)


def dot(a, b, ca, cb):
    return lax.dot_general(a, b, (((ca,), (cb,)), ((), ())), preferred_element_type=F32)


def tiles(g, scan):
    return HG + (1 if scan == 1 and g == G - 1 else 0)


def scratch_shapes():
    shapes = {}
    for name in ("q", "k", "v", "dy"):
        shapes[name] = pltpu.VMEM((TOK, F), BF16)
    shapes["gain"] = pltpu.VMEM((1, F), F32)
    shapes["load_sem"] = pltpu.SemaphoreType.DMA((5,))
    for s in range(2):
        for g in range(G):
            n = tiles(g, s)
            shapes[f"own{s}{g}"] = pltpu.VMEM((2, CHIPS, n, 8, HD), F32)
            for name in ("pair", "sums", "gath", "give", "back", "hand", "taken"):
                shapes[f"{name}{s}{g}"] = pltpu.VMEM((CHIPS, n, 8, HD), F32)
        for name in ("out_s", "out_r", "back_s", "back_r"):
            shapes[f"{name}{s}"] = pltpu.SemaphoreType.DMA((G, N_OFF))
        for name in ("pair_s", "pair_r", "hand_s", "hand_r"):
            shapes[f"{name}{s}"] = pltpu.SemaphoreType.DMA((G,))
    shapes["prefix"] = pltpu.VMEM((HEADS, HD, HD), BF16)
    shapes["masked"] = pltpu.VMEM((HEADS, TOK, TOK), BF16)
    shapes["qt"] = pltpu.VMEM((HEADS, HD, TOK), BF16)
    shapes["attn"] = pltpu.VMEM((TOK, F), F32)
    shapes["dnorm"] = pltpu.VMEM((TOK, F), F32)
    shapes["grad"] = pltpu.VMEM((TOK, F), BF16)
    shapes["gk_part"] = pltpu.VMEM((TOK, F), F32)
    shapes["gv_part"] = pltpu.VMEM((TOK, F), F32)
    shapes["zrow"] = pltpu.VMEM((DP, 8, HD), F32)
    shapes["ztile"] = pltpu.VMEM((8, HD), F32)
    shapes["gtile"] = pltpu.VMEM((8, HD), F32)
    shapes["gback"] = pltpu.VMEM((CHIPS, 8, HD), F32)
    shapes["gtaken"] = pltpu.VMEM((CHIPS, 8, HD), F32)
    shapes["z_s"] = pltpu.SemaphoreType.DMA((DP - 1,))
    shapes["z_r"] = pltpu.SemaphoreType.DMA((DP - 1,))
    shapes["gb_s"] = pltpu.SemaphoreType.DMA((N_OFF,))
    shapes["gb_r"] = pltpu.SemaphoreType.DMA((N_OFF,))
    shapes["gp_s"] = pltpu.SemaphoreType.DMA((1,))
    shapes["gp_r"] = pltpu.SemaphoreType.DMA((1,))
    return shapes


NAMES = list(scratch_shapes())


def kernel(q_hbm, k_hbm, v_hbm, dy_hbm, gain_hbm, gq_ref, gk_ref, gv_ref, gg_ref, *scratch):
    m = dict(zip(NAMES, scratch))
    q, k, v, dy, gain = (m[n] for n in ("q", "k", "v", "dy", "gain"))
    loads = [
        pltpu.make_async_copy(src, dst, m["load_sem"].at[i])
        for i, (src, dst) in enumerate(((k_hbm, k), (v_hbm, v), (q_hbm, q), (dy_hbm, dy), (gain_hbm, gain)))
    ]
    for load in loads:
        load.start()

    z = lax.axis_index("dp")
    s_at = lax.axis_index("seq")
    chip = s_at // 2
    core = s_at % 2
    other = 1 - core
    y, x = chip // SIDE, chip % SIDE

    partner = (z, chip * 2 + other)
    near = [((y + dy_) % SIDE) * SIDE + (x + dx_) % SIDE for dy_, dx_ in OFFSETS]
    targets = [(z, c * 2 + core) for c in near]
    z_targets = [((z + d) % DP, s_at) for d in range(1, DP)]

    barrier = pltpu.get_barrier_semaphore()
    for t in [partner] + targets + z_targets:
        pl.semaphore_signal(barrier, inc=1, device_id=t, device_id_type=MESH)

    pending = []

    def remote(src, dst, ssem, rsem, target):
        copy = pltpu.make_async_remote_copy(
            src_ref=src, dst_ref=dst, send_sem=ssem, recv_sem=rsem, device_id=target, device_id_type=MESH
        )
        copy.start()
        pending.append(copy)
        return copy

    def lanes(head):
        return pl.ds(pl.multiple_of(head * HD, HD), HD)

    def each_head(first, count, step, body):
        def some(i, carry):
            for j in range(step):
                body(first + i * step + j, i * step + j)
            return carry

        lax.fori_loop(0, count // step, some, 0)

    def tile3(value):
        return value.reshape(CHIPS, 8, HD)

    def pair_send(scan, g):
        return remote(
            m[f"own{scan}{g}"].at[other], m[f"pair{scan}{g}"], m[f"pair_s{scan}"].at[g], m[f"pair_r{scan}"].at[g], partner
        )

    def out_send(scan, g):
        sums, gath = m[f"sums{scan}{g}"], m[f"gath{scan}{g}"]

        def add(c, carry):
            sums[c] = m[f"own{scan}{g}"][core, c] + m[f"pair{scan}{g}"][c]
            return carry

        lax.fori_loop(0, CHIPS, add, 0)
        gath[chip] = sums[chip]
        return [
            remote(sums.at[near[i]], gath.at[chip], m[f"out_s{scan}"].at[g, i], m[f"out_r{scan}"].at[g, i], targets[i])
            for i in range(N_OFF)
        ]

    def back_send(scan, g):
        gath, give, back = m[f"gath{scan}{g}"], m[f"give{scan}{g}"], m[f"back{scan}{g}"]

        def one(t, carry):
            total = jnp.zeros((8, HD), F32)
            for c in range(CHIPS) if scan == 0 else reversed(range(CHIPS)):
                give[c, t] = total
                total = total + gath[c, t]
            return carry

        lax.fori_loop(0, HG, one, 0)
        back[chip, :HG] = give[chip, :HG]
        return [
            remote(
                give.at[near[i], pl.ds(0, HG)],
                back.at[chip, pl.ds(0, HG)],
                m[f"back_s{scan}"].at[g, i],
                m[f"back_r{scan}"].at[g, i],
                targets[i],
            )
            for i in range(N_OFF)
        ]

    def hand_send(scan, g):
        hand = m[f"hand{scan}{g}"]
        with_own = jnp.where(core == (0 if scan == 0 else 1), 1.0, 0.0).astype(F32)

        def add(c, carry):
            hand[c, :HG] = m[f"back{scan}{g}"][c, :HG] + m[f"own{scan}{g}"][core, c, :HG] * with_own
            return carry

        lax.fori_loop(0, CHIPS, add, 0)
        return remote(
            hand.at[:, pl.ds(0, HG)],
            m[f"taken{scan}{g}"].at[:, pl.ds(0, HG)],
            m[f"hand_s{scan}"].at[g],
            m[f"hand_r{scan}"].at[g],
            partner,
        )

    def carried(scan, g, j, mine):
        if mine:
            with_pair = jnp.where(core == (1 if scan == 0 else 0), 1.0, 0.0).astype(F32)
            value = m[f"back{scan}{g}"][:, j] + m[f"pair{scan}{g}"][:, j] * with_pair
        else:
            value = m[f"taken{scan}{g}"][:, j]
        return value.reshape(HD, HD).astype(BF16)

    def states(half, g):
        def body(head, j):
            at = lanes(head)
            m[f"own0{g}"][half, :, j] = tile3(dot(k[:, at], v[:, at], 0, 0))

        each_head(half * HALF + g * HG, HG, 4, body)

    loads[0].wait()
    loads[1].wait()
    states(other, 0)
    pl.semaphore_wait(barrier, 1 + N_OFF + DP - 1)
    pairs = [pair_send(0, 0)]
    for g in range(1, G):
        states(other, g)
        pairs.append(pair_send(0, g))
    outs = []
    for g in range(G):
        states(core, g)
        pairs[g].wait_recv()
        outs.append(out_send(0, g))
    for load in loads[2:]:
        load.wait()

    rows = lax.broadcasted_iota(jnp.int32, (TOK, TOK), 0)
    cols = lax.broadcasted_iota(jnp.int32, (TOK, TOK), 1)
    causal = rows >= cols

    def local_part(head, j):
        at = lanes(head)
        q_h = q[:, at]
        scores = jnp.where(causal, dot(q_h, k[:, at], 1, 1), 0.0).astype(BF16)
        m["masked"][head] = scores
        m["attn"][:, at] = dot(scores, v[:, at], 1, 0)
        m["dnorm"][:, at] = dy[:, at].astype(F32) * gain[:, at]
        m["qt"][head] = q_h.T

    backs = []
    for g in range(G):
        each_head(g * (HEADS // G), HEADS // G, 4, local_part)
        for copy in outs[g]:
            copy.wait_recv()
        backs.append(back_send(0, g))
    hands = []
    for g in range(G):
        for copy in backs[g]:
            copy.wait_recv()
        hands.append(hand_send(0, g))

    sq = jnp.zeros((TOK, HD), F32)
    cross = jnp.zeros((TOK, HD), F32)

    def attn_part(half, g, mine, acc):
        def some(i, acc):
            sq, cross = acc
            for u in range(4):
                j = i * 4 + u
                head = half * HALF + g * HG + j
                at = lanes(head)
                p = carried(0, g, j, mine)
                m["prefix"][head] = p
                a = m["attn"][:, at] + dot(q[:, at], p, 1, 0)
                m["attn"][:, at] = a
                sq = sq + a * a
                cross = cross + a * m["dnorm"][:, at]
            return (sq, cross)

        return lax.fori_loop(0, HG // 4, some, acc)

    acc = (sq, cross)
    for g in range(G):
        acc = attn_part(core, g, True, acc)
    for g in range(G):
        hands[g].wait_recv()
        acc = attn_part(other, g, False, acc)
    sq, cross = acc
    scale = lax.rsqrt(jnp.sum(sq, axis=1, keepdims=True) * (1.0 / F) + 1e-06)
    inner = scale * (jnp.sum(cross, axis=1, keepdims=True) * (1.0 / F))
    scale = jnp.broadcast_to(scale, (TOK, HD))
    inner = jnp.broadcast_to(inner, (TOK, HD))

    def gstates(half, g):
        def body(head, j):
            at = lanes(head)
            normed = m["attn"][:, at] * scale
            grad = (scale * (m["dnorm"][:, at] - normed * inner)).astype(BF16)
            m["grad"][:, at] = grad
            term = tile3(dy[:, at].astype(F32) * normed).sum(axis=0)
            m[f"own1{G - 1}"][half, g * HG + j, HG] = term
            m[f"own1{g}"][half, :, j] = tile3(dot(m["qt"][head], grad, 1, 0))

        each_head(half * HALF + g * HG, HG, 4, body)

    pairs = []
    for g in range(G):
        gstates(other, g)
        pairs.append(pair_send(1, g))
    outs = []
    for g in range(G):
        gstates(core, g)
        pairs[g].wait_recv()
        outs.append(out_send(1, g))

    def grads_part(head, j):
        at = lanes(head)
        q_h, k_h, v_h, g_h = q[:, at], k[:, at], v[:, at], m["grad"][:, at]
        dmask = jnp.where(causal, dot(g_h, v_h, 1, 1), 0.0).astype(BF16)
        gq_ref[:, at] = (dot(dmask, k_h, 1, 0) + dot(g_h, m["prefix"][head], 1, 1)).astype(BF16)
        m["gk_part"][:, at] = dot(dmask, q_h, 0, 0)
        m["gv_part"][:, at] = dot(m["masked"][head], g_h, 0, 0)

    backs = []
    for g in range(G):
        each_head(g * (HEADS // G), HEADS // G, 4, grads_part)
        for copy in outs[g]:
            copy.wait_recv()
        if g == G - 1:
            gath = m[f"gath1{g}"]
            total = gath[0, HG]
            for c in range(1, CHIPS):
                total = total + gath[c, HG]
            m["ztile"][...] = total
            m["zrow"][z] = total
            zs = [
                remote(m["ztile"], m["zrow"].at[z], m["z_s"].at[i], m["z_r"].at[i], z_targets[i])
                for i in range(DP - 1)
            ]
        backs.append(back_send(1, g))

    for copy in zs:
        copy.wait_recv()
    total = m["zrow"][0]
    for i in range(1, DP):
        total = total + m["zrow"][i]
    total = jnp.sum(total, axis=0, keepdims=True) * (1.0 / math.sqrt(DP * 32 * TOK))
    total = jnp.broadcast_to(total, (8, HD))
    m["gtile"][...] = total
    m["gback"][chip] = total
    gbs = [
        remote(m["gtile"], m["gback"].at[chip], m["gb_s"].at[i], m["gb_r"].at[i], targets[i]) for i in range(N_OFF)
    ]

    hands = []
    for g in range(G):
        for copy in backs[g]:
            copy.wait_recv()
        hands.append(hand_send(1, g))

    def finish(half, g, mine):
        def body(head, j):
            at = lanes(head)
            s = carried(1, g, j, mine)
            gk_ref[:, at] = (m["gk_part"][:, at] + dot(v[:, at], s, 1, 1)).astype(BF16)
            gv_ref[:, at] = (m["gv_part"][:, at] + dot(k[:, at], s, 1, 0)).astype(BF16)

        each_head(half * HALF + g * HG, HG, 4, body)

    for g in range(G):
        finish(core, g, True)
    for copy in gbs:
        copy.wait_recv()
    gp = remote(m["gback"], m["gtaken"], m["gp_s"].at[0], m["gp_r"].at[0], partner)
    for g in range(G):
        hands[g].wait_recv()
        finish(other, g, False)
    gp.wait_recv()
    gg_ref[pl.ds(core * HALF, HALF)] = m["gback"][:, 0, :]
    gg_ref[pl.ds(other * HALF, HALF)] = m["gtaken"][:, 0, :]
    for copy in pending:
        copy.wait_send()


def shards(query, key_in, value_in, cotangent, gain):
    out = jax.ShapeDtypeStruct((TOK, F), BF16)
    vmem = pl.BlockSpec(memory_space=pltpu.VMEM)
    shapes = scratch_shapes()
    gq, gk, gv, gg = pl.pallas_call(
        kernel,
        out_shape=(out, out, out, jax.ShapeDtypeStruct((HEADS, HD), F32)),
        in_specs=[pl.BlockSpec(memory_space=pl.ANY)] * 5,
        out_specs=(vmem, vmem, vmem, vmem),
        scratch_shapes=[shapes[n] for n in NAMES],
        compiler_params=pltpu.CompilerParams(
            collective_id=0, has_side_effects=True, vmem_limit_bytes=60 * 2**20
        ),
        name="scan_grads",
    )(query[0], key_in[0], value_in[0], cotangent[0], gain.reshape(1, F))
    return gq[None], gk[None], gv[None], gg.reshape(F)


def solution(mesh):
    placed = P("dp", "seq", None)
    return jax.shard_map(
        shards,
        mesh=mesh,
        in_specs=(placed, placed, placed, placed, P()),
        out_specs=(placed, placed, placed, P()),
        check_vma=False,
    )
```

time: 658 us -> 83.9 us (0.13)
  waiting for transfers between devices: 316 us -> 0 us
  other arithmetic: 147 us -> 0 us
  blocking collectives: 77.8 us -> 0 us
  Pallas kernels: 0 us -> 77.5 us
  local copies, waits for them, and re-layouts: 66 us -> 5.56 us
  matrix products: 32.5 us -> 0 us
  between operations: 14.3 us -> 0.65 us
    all_gather x2 -> x0, waiting for transfers between devices: 316 us -> none  [carried_in(): pieces = lax.all_gather(value, axis)]
    select_n x62 -> x0, other arithmetic: 143 us -> none  [step(): return jnp.where(position < mine, longer, running)]
    psum x1 -> x0, blocking collectives: 77.8 us -> none  [shards(): gain_sum = lax.psum(jnp.sum(dy_f * normed, axis=0), ('dp', 'seq'))]
    pallas_call x0 -> x1, Pallas kernels: none -> 77.5 us  [shards(): pl.pallas_call(kernel, out_shape=(out, out, out, jax.ShapeDtypeStruct((HE...]
    rev x1 -> x0, local copies, waits for them, and re-layouts: 43.8 us -> none  [carried_in(): pieces = pieces[::-1]]
    dot_general x16 -> x0, matrix products: 32.5 us -> none  [the longest x4 7.99 us: state_product(): jnp.einsum(form, data, lower, preferred_element_type=jnp.float32)]
    unnamed x46 -> x10, local copies, waits for them, and re-layouts: 13.6 us -> 5.56 us
  transfers between devices with their start and end apart: 2 -> 0, of which waited for: 2 -> 0; matrix products, arithmetic and copies ran while one was open for 3% -> 0% of each run, Pallas kernels for 0% -> 0%
where the time goes in v1:
time: 83.9 us; the launch traced here: 83.7 us
  Pallas kernels  77.5 us (92%)
  local copies, waits for them, and re-layouts  5.56 us (7%)
    pallas_call x1, Pallas kernels, shards(): pl.pallas_call(kernel, out_shape=(out, out, out, jax.ShapeDtypeStruct((HE...  77.5 us
    unnamed x10, local copies, waits for them, and re-layouts  5.56 us

profile of v1, /device:TPU:1, one launch (start us, length us, event | category | flops | bytes accessed | tf_op | source)
XLA Modules:
  0.0 83.7 jit_solution(4308130823196298592)
XLA Ops:
  0.6 77.5 %scan_grads.1 = (bf16[128,4096]{1,0:T(8,128)(2,1)}, bf16[128,4096]{1,0:T(8,128)(2,1)}, bf16[128,4096]{1,0:T(8,128)(2,1)}, f32[32,128]{1,0:T(8,128)}) custom-call(bf16[128,4096]{1,0:T(8,128)(2,1)} %bitcast.12, bf16[128,4096]{1,0:T(8,128)(2,1)} %bitcast.13, bf16[128,4096]{1,0:T(8,128)(2,1)} %bitcast.14, bf16[128,4096]{1,0:T(8,128)(2,1)} %bitcast.15, ...), custom_call_target="tpu_custom_call" | custom-call | tf_op jit(solution)/shard_map/scan_grads/pallas_call | solution.py:370
  78.2 0.0 copy-start.1
  78.2 2.4 %copy.13 = bf16[1,128,4096]{2,1,0:T(8,128)(2,1)} copy(bf16[1,128,4096]{2,1,0:T(8,128)(2,1)} %bitcast.11) | data formatting | bytes 2097152
  80.5 0.0 copy-done.1
  80.5 0.0 copy-start
  80.5 1.0 %copy.14 = bf16[1,128,4096]{2,1,0:T(8,128)(2,1)} copy(bf16[1,128,4096]{2,1,0:T(8,128)(2,1)S(1)} %bitcast.10) | data formatting | bytes 2097152
  81.5 0.6 copy-done
  82.1 0.0 copy-start.2
  82.1 1.0 %copy.15 = bf16[1,128,4096]{2,1,0:T(8,128)(2,1)} copy(bf16[1,128,4096]{2,1,0:T(8,128)(2,1)S(1)} %bitcast.9) | data formatting | bytes 2097152
  83.1 0.0 copy-done.2
  83.1 0.6 copy.16
Async XLA Ops:
  78.2 2.4 %copy-start.1 = (bf16[128,4096]{1,0:T(8,128)(2,1)S(1)}, bf16[128,4096]{1,0:T(8,128)(2,1)}, u32[]{:S(2)}) copy-start(bf16[128,4096]{1,0:T(8,128)(2,1)} %get-tuple-element.9) | copy-start | bytes 3145732
  80.5 1.6 %copy-start = (bf16[128,4096]{1,0:T(8,128)(2,1)S(1)}, bf16[128,4096]{1,0:T(8,128)(2,1)}, u32[]{:S(2)}) copy-start(bf16[128,4096]{1,0:T(8,128)(2,1)} %get-tuple-element.10) | copy-start | bytes 3145732
  82.1 1.0 %copy-start.2 = (f32[32,128]{1,0:T(8,128)S(1)}, f32[32,128]{1,0:T(8,128)}, u32[]{:S(2)}) copy-start(f32[32,128]{1,0:T(8,128)} %get-tuple-element.11) | copy-start | bytes 49156

commit v2 on v1

v2 whole, which is shorter than its diff:
```python
import functools
import math

import jax
import jax.numpy as jnp
from jax import lax
from jax.experimental import pallas as pl
from jax.experimental.pallas import tpu as pltpu
from jax.sharding import PartitionSpec as P

HD = 128
TOK = 128
HEADS = 32
F = HEADS * HD
HALF = HEADS // 2
SIDE = 4
CHIPS = SIDE * SIDE
DP = 8
GROUPS = (8, 8)
G = len(GROUPS)
FIRST = [sum(GROUPS[:g]) for g in range(G)]
MESH = pl.DeviceIdType.MESH
F32 = jnp.float32
BF16 = jnp.bfloat16

OFFSETS = [(dy, dx) for dy in range(SIDE) for dx in range(SIDE) if (dy, dx) != (0, 0)]
N_OFF = len(OFFSETS)


def dot(a, b, ca, cb):
    return lax.dot_general(a, b, (((ca,), (cb,)), ((), ())), preferred_element_type=F32)


def tiles(g, scan):
    return GROUPS[g] + (1 if scan == 1 and g == G - 1 else 0)


def scratch_shapes():
    shapes = {}
    for name in ("q", "k", "v", "dy"):
        shapes[name] = pltpu.VMEM((TOK, F), BF16)
    shapes["gain"] = pltpu.VMEM((1, F), F32)
    shapes["load_sem"] = pltpu.SemaphoreType.DMA((5,))
    for s in range(2):
        for g in range(G):
            n = tiles(g, s)
            shapes[f"own{s}{g}"] = pltpu.VMEM((2, CHIPS, n, 8, HD), F32)
            for name in ("pair", "sums", "gath", "give", "back", "hand", "taken"):
                shapes[f"{name}{s}{g}"] = pltpu.VMEM((CHIPS, n, 8, HD), F32)
        for name in ("out_s", "out_r", "back_s", "back_r", "pair_s", "pair_r", "hand_s", "hand_r"):
            shapes[f"{name}{s}"] = pltpu.SemaphoreType.DMA((G,))
    shapes["prefix"] = pltpu.VMEM((HEADS, HD, HD), BF16)
    shapes["masked"] = pltpu.VMEM((HEADS, TOK, TOK), BF16)
    shapes["qt"] = pltpu.VMEM((HEADS, HD, TOK), BF16)
    shapes["attn"] = pltpu.VMEM((TOK, F), F32)
    shapes["dnorm"] = pltpu.VMEM((TOK, F), F32)
    shapes["grad"] = pltpu.VMEM((TOK, F), BF16)
    shapes["gk_part"] = pltpu.VMEM((TOK, F), F32)
    shapes["gv_part"] = pltpu.VMEM((TOK, F), F32)
    shapes["zrow"] = pltpu.VMEM((DP, 8, HD), F32)
    shapes["ztile"] = pltpu.VMEM((8, HD), F32)
    shapes["gtile"] = pltpu.VMEM((8, HD), F32)
    shapes["gback"] = pltpu.VMEM((CHIPS, 8, HD), F32)
    shapes["gtaken"] = pltpu.VMEM((CHIPS, 8, HD), F32)
    for name in ("z_s", "z_r", "gb_s", "gb_r", "gp_s", "gp_r"):
        shapes[name] = pltpu.SemaphoreType.DMA((1,))
    return shapes


NAMES = list(scratch_shapes())


def kernel(q_hbm, k_hbm, v_hbm, dy_hbm, gain_hbm, gq_ref, gk_ref, gv_ref, gg_ref, *scratch):
    m = dict(zip(NAMES, scratch))
    q, k, v, dy, gain = (m[n] for n in ("q", "k", "v", "dy", "gain"))
    loads = [
        pltpu.make_async_copy(src, dst, m["load_sem"].at[i])
        for i, (src, dst) in enumerate(((k_hbm, k), (v_hbm, v), (q_hbm, q), (dy_hbm, dy), (gain_hbm, gain)))
    ]
    for load in loads:
        load.start()

    z = lax.axis_index("dp")
    s_at = lax.axis_index("seq")
    chip = s_at // 2
    core = s_at % 2
    other = 1 - core
    y, x = chip // SIDE, chip % SIDE

    partner = (z, chip * 2 + other)
    near = [((y + dy_) % SIDE) * SIDE + (x + dx_) % SIDE for dy_, dx_ in OFFSETS]
    targets = [(z, c * 2 + core) for c in near]
    z_targets = [((z + d) % DP, s_at) for d in range(1, DP)]

    barrier = pltpu.get_barrier_semaphore()
    for t in [partner] + targets + z_targets:
        pl.semaphore_signal(barrier, inc=1, device_id=t, device_id_type=MESH)

    pending = []

    def wait_bytes(ref, sem):
        pltpu.make_async_copy(ref, ref, sem).wait()

    def remote(src, dst, ssem, rsem, target):
        copy = pltpu.make_async_remote_copy(
            src_ref=src, dst_ref=dst, send_sem=ssem, recv_sem=rsem, device_id=target, device_id_type=MESH
        )
        copy.start()
        return copy

    def fan(src_of, dst, ssem, rsem, to, whole):
        for i, target in enumerate(to):
            remote(src_of(i), dst, ssem, rsem, target)
        pending.append(lambda: wait_bytes(whole, ssem))
        return lambda: wait_bytes(whole, rsem)

    def to_partner(src, dst, ssem, rsem):
        copy = remote(src, dst, ssem, rsem, partner)
        pending.append(copy.wait_send)
        return copy.wait_recv

    def lanes(head):
        return pl.ds(pl.multiple_of(head * HD, HD), HD)

    def each_head(first, count, body, carry=0):
        step = 4 if count % 4 == 0 else 2

        def some(i, carry):
            for u in range(step):
                carry = body(first + i * step + u, i * step + u, carry)
            return carry

        return lax.fori_loop(0, count // step, some, carry)

    def tile3(value):
        return value.reshape(CHIPS, 8, HD)

    def pair_send(scan, g):
        return to_partner(
            m[f"own{scan}{g}"].at[other], m[f"pair{scan}{g}"], m[f"pair_s{scan}"].at[g], m[f"pair_r{scan}"].at[g]
        )

    def out_send(scan, g):
        sums, gath = m[f"sums{scan}{g}"], m[f"gath{scan}{g}"]

        def add(c, carry):
            sums[c] = m[f"own{scan}{g}"][core, c] + m[f"pair{scan}{g}"][c]
            return carry

        lax.fori_loop(0, CHIPS, add, 0)
        gath[chip] = sums[chip]
        return fan(
            lambda i: sums.at[near[i]],
            gath.at[chip],
            m[f"out_s{scan}"].at[g],
            m[f"out_r{scan}"].at[g],
            targets,
            gath.at[pl.ds(0, N_OFF)],
        )

    def back_send(scan, g):
        gath, give, back = m[f"gath{scan}{g}"], m[f"give{scan}{g}"], m[f"back{scan}{g}"]

        def one(t, carry):
            total = jnp.zeros((8, HD), F32)
            for c in range(CHIPS) if scan == 0 else reversed(range(CHIPS)):
                give[c, t] = total
                total = total + gath[c, t]
            return carry

        lax.fori_loop(0, GROUPS[g], one, 0)
        back[chip, :GROUPS[g]] = give[chip, :GROUPS[g]]
        heads = pl.ds(0, GROUPS[g])
        return fan(
            lambda i: give.at[near[i], heads],
            back.at[chip, heads],
            m[f"back_s{scan}"].at[g],
            m[f"back_r{scan}"].at[g],
            targets,
            back.at[pl.ds(0, N_OFF), heads],
        )

    def hand_send(scan, g):
        hand = m[f"hand{scan}{g}"]
        with_own = jnp.where(core == (0 if scan == 0 else 1), 1.0, 0.0).astype(F32)

        def add(c, carry):
            hand[c, :GROUPS[g]] = m[f"back{scan}{g}"][c, :GROUPS[g]] + m[f"own{scan}{g}"][core, c, :GROUPS[g]] * with_own
            return carry

        lax.fori_loop(0, CHIPS, add, 0)
        return to_partner(
            hand.at[:, pl.ds(0, GROUPS[g])],
            m[f"taken{scan}{g}"].at[:, pl.ds(0, GROUPS[g])],
            m[f"hand_s{scan}"].at[g],
            m[f"hand_r{scan}"].at[g],
        )

    def carried(scan, g, j, mine):
        if mine:
            with_pair = jnp.where(core == (1 if scan == 0 else 0), 1.0, 0.0).astype(F32)
            value = m[f"back{scan}{g}"][:, j] + m[f"pair{scan}{g}"][:, j] * with_pair
        else:
            value = m[f"taken{scan}{g}"][:, j]
        return value.reshape(HD, HD).astype(BF16)

    def states(half, g):
        def body(head, j, carry):
            at = lanes(head)
            m[f"own0{g}"][half, :, j] = tile3(dot(k[:, at], v[:, at], 0, 0))
            return carry

        each_head(half * HALF + FIRST[g], GROUPS[g], body)

    loads[0].wait()
    loads[1].wait()
    for g in range(G):
        states(other, g)
    states(core, 0)
    pl.semaphore_wait(barrier, 1 + N_OFF + DP - 1)
    pairs = [pair_send(0, g) for g in range(G)]
    for g in range(1, G):
        states(core, g)
    outs = []
    for g in range(G):
        pairs[g]()
        outs.append(out_send(0, g))
    for load in loads[2:]:
        load.wait()

    rows = lax.broadcasted_iota(jnp.int32, (TOK, TOK), 0)
    cols = lax.broadcasted_iota(jnp.int32, (TOK, TOK), 1)
    causal = rows >= cols

    def local_part(head, j, carry):
        at = lanes(head)
        scores = jnp.where(causal, dot(q[:, at], k[:, at], 1, 1), 0.0).astype(BF16)
        m["masked"][head] = scores
        m["attn"][:, at] = dot(scores, v[:, at], 1, 0)
        return carry

    def later_part(head, j, carry):
        at = lanes(head)
        m["dnorm"][:, at] = dy[:, at].astype(F32) * gain[:, at]
        m["qt"][head] = q[:, at].T
        return carry

    backs = []
    for g in range(G):
        each_head(2 * FIRST[g], 2 * GROUPS[g], local_part)
        outs[g]()
        backs.append(back_send(0, g))
    each_head(0, HEADS, later_part)

    def attn_part(half, g, mine, acc):
        def body(head, j, acc):
            sq, cross = acc
            at = lanes(head)
            p = carried(0, g, j, mine)
            m["prefix"][head] = p
            a = m["attn"][:, at] + dot(q[:, at], p, 1, 0)
            m["attn"][:, at] = a
            return (sq + a * a, cross + a * m["dnorm"][:, at])

        return each_head(half * HALF + FIRST[g], GROUPS[g], body, acc)

    acc = (jnp.zeros((TOK, HD), F32), jnp.zeros((TOK, HD), F32))
    for g in range(G):
        backs[g]()
        hand = hand_send(0, g)
        acc = attn_part(core, g, True, acc)
        hand()
        acc = attn_part(other, g, False, acc)
    sq, cross = acc
    scale = lax.rsqrt(jnp.sum(sq, axis=1, keepdims=True) * (1.0 / F) + 1e-06)
    inner = scale * (jnp.sum(cross, axis=1, keepdims=True) * (1.0 / F))
    scale = jnp.broadcast_to(scale, (TOK, HD))
    inner = jnp.broadcast_to(inner, (TOK, HD))

    def gstates(half, g):
        def body(head, j, carry):
            at = lanes(head)
            normed = m["attn"][:, at] * scale
            grad = (scale * (m["dnorm"][:, at] - normed * inner)).astype(BF16)
            m["grad"][:, at] = grad
            term = tile3(dy[:, at].astype(F32) * normed).sum(axis=0)
            m[f"own1{G - 1}"][half, FIRST[g] + j, GROUPS[G - 1]] = term
            m[f"own1{g}"][half, :, j] = tile3(dot(m["qt"][head], grad, 1, 0))
            return carry

        each_head(half * HALF + FIRST[g], GROUPS[g], body)

    pairs = []
    for g in range(G):
        gstates(other, g)
        pairs.append(pair_send(1, g))
    outs = []
    for g in range(G):
        gstates(core, g)
        pairs[g]()
        outs.append(out_send(1, g))

    def grads_part(head, j, carry):
        at = lanes(head)
        g_h = m["grad"][:, at]
        dmask = jnp.where(causal, dot(g_h, v[:, at], 1, 1), 0.0).astype(BF16)
        gq_ref[:, at] = (dot(dmask, k[:, at], 1, 0) + dot(g_h, m["prefix"][head], 1, 1)).astype(BF16)
        m["gk_part"][:, at] = dot(dmask, q[:, at], 0, 0)
        return carry

    def value_part(head, j, carry):
        at = lanes(head)
        m["gv_part"][:, at] = dot(m["masked"][head], m["grad"][:, at], 0, 0)
        return carry

    backs = []
    for g in range(G):
        each_head(2 * FIRST[g], 2 * GROUPS[g], grads_part)
        outs[g]()
        if g == G - 1:
            gath = m[f"gath1{g}"]
            total = gath[0, GROUPS[g]]
            for c in range(1, CHIPS):
                total = total + gath[c, GROUPS[g]]
            m["ztile"][...] = total
            m["zrow"][z] = total
            zs = fan(
                lambda i: m["ztile"], m["zrow"].at[z], m["z_s"].at[0], m["z_r"].at[0], z_targets, m["zrow"].at[pl.ds(0, DP - 1)]
            )
        backs.append(back_send(1, g))
    each_head(0, HEADS, value_part)

    def finish(half, g, mine):
        def body(head, j, carry):
            at = lanes(head)
            s = carried(1, g, j, mine)
            gk_ref[:, at] = (m["gk_part"][:, at] + dot(v[:, at], s, 1, 1)).astype(BF16)
            gv_ref[:, at] = (m["gv_part"][:, at] + dot(k[:, at], s, 1, 0)).astype(BF16)
            return carry

        each_head(half * HALF + FIRST[g], GROUPS[g], body)

    for g in range(G):
        if g == G - 1:
            zs()
            total = m["zrow"][0]
            for i in range(1, DP):
                total = total + m["zrow"][i]
            total = jnp.sum(total, axis=0, keepdims=True) * (1.0 / math.sqrt(DP * 32 * TOK))
            total = jnp.broadcast_to(total, (8, HD))
            m["gtile"][...] = total
            m["gback"][chip] = total
            gbs = fan(
                lambda i: m["gtile"], m["gback"].at[chip], m["gb_s"].at[0], m["gb_r"].at[0], targets, m["gback"].at[pl.ds(0, N_OFF)]
            )
        backs[g]()
        hand = hand_send(1, g)
        finish(core, g, True)
        if g == G - 1:
            gbs()
            gp = to_partner(m["gback"], m["gtaken"], m["gp_s"].at[0], m["gp_r"].at[0])
        hand()
        finish(other, g, False)
    gg_ref[pl.ds(core * HALF, HALF)] = m["gback"][:, 0, :]
    gp()
    gg_ref[pl.ds(other * HALF, HALF)] = m["gtaken"][:, 0, :]
    for wait in pending:
        wait()


def write_out(*refs):
    ins, outs, sem = refs[:4], refs[4:8], refs[8]
    copies = [pltpu.make_async_copy(i, o, sem.at[n]) for n, (i, o) in enumerate(zip(ins, outs))]
    for copy in copies:
        copy.start()
    for copy in copies:
        copy.wait()


def shards(query, key_in, value_in, cotangent, gain):
    shapes = scratch_shapes()
    vmem = pl.BlockSpec(memory_space=pltpu.VMEM)
    hbm = pl.BlockSpec(memory_space=pl.ANY)
    kept = (pltpu.VMEM((TOK, F), BF16),) * 3 + (pltpu.VMEM((HEADS, HD), F32),)
    results = pl.pallas_call(
        kernel,
        out_shape=kept,
        in_specs=[hbm] * 5,
        out_specs=(vmem,) * 4,
        scratch_shapes=[shapes[n] for n in NAMES],
        compiler_params=pltpu.CompilerParams(
            collective_id=0, has_side_effects=True, vmem_limit_bytes=60 * 2**20
        ),
        name="scan_grads",
    )(query[0], key_in[0], value_in[0], cotangent[0], gain.reshape(1, F))
    gq, gk, gv, gg = pl.pallas_call(
        write_out,
        out_shape=tuple(jax.ShapeDtypeStruct(r.shape, r.dtype) for r in results),
        in_specs=[vmem] * 4,
        out_specs=(hbm,) * 4,
        scratch_shapes=[pltpu.SemaphoreType.DMA((4,))],
        compiler_params=pltpu.CompilerParams(vmem_limit_bytes=8 * 2**20),
        name="write_out",
    )(*results)
    return gq[None], gk[None], gv[None], gg.reshape(F)


def solution(mesh):
    placed = P("dp", "seq", None)
    return jax.shard_map(
        shards,
        mesh=mesh,
        in_specs=(placed, placed, placed, placed, P()),
        out_specs=(placed, placed, placed, P()),
        check_vma=False,
    )
```

time: 83.9 us -> 75.4 us (0.90)
  local copies, waits for them, and re-layouts: 5.56 us -> 0 us
  Pallas kernels: 77.5 us -> 74.7 us
    unnamed x10 -> x0, local copies, waits for them, and re-layouts: 5.56 us -> none
    pallas_call x1 -> x2, Pallas kernels: 77.5 us -> 74.7 us  [the longest x1 73 us: shards(): pl.pallas_call(kernel, out_shape=kept, in_specs=[hbm] * 5, out_specs=(vme...]
where the time goes in v2:
time: 75.4 us; the launch traced here: 75.3 us
  Pallas kernels  74.7 us (99%)
    pallas_call x1, Pallas kernels, shards(): pl.pallas_call(kernel, out_shape=kept, in_specs=[hbm] * 5, out_specs=(vme...  73 us
    pallas_call x1, Pallas kernels, shards(): pl.pallas_call(write_out, out_shape=tuple((jax.ShapeDtypeStruct(r.shape,...  1.7 us

profile of v2, /device:TPU:1, one launch (start us, length us, event | category | flops | bytes accessed | tf_op | source)
XLA Modules:
  0.0 75.3 jit_solution(17381729971608827045)
XLA Ops:
  0.6 73.0 %scan_grads.1 = (bf16[128,4096]{1,0:T(8,128)(2,1)S(1)}, bf16[128,4096]{1,0:T(8,128)(2,1)S(1)}, bf16[128,4096]{1,0:T(8,128)(2,1)S(1)}, f32[32,128]{1,0:T(8,128)S(1)}) custom-call(bf16[128,4096]{1,0:T(8,128)(2,1)} %bitcast.9, bf16[128,4096]{1,0:T(8,128)(2,1)} %bitcast.10, bf16[128,4096]{1,0:T(8,128)(2,1)} %bitcast.11, bf16[128,4096]{1,0:T(8,128)(2,1)} %bitcast.12, ...), custom_call_target="tpu_custom_call" | custom-call | tf_op jit(solution)/shard_map/scan_grads/pallas_call | solution.py:385
  73.6 1.7 %write_out.1 = (bf16[128,4096]{1,0:T(8,128)(2,1)}, bf16[128,4096]{1,0:T(8,128)(2,1)}, bf16[128,4096]{1,0:T(8,128)(2,1)}, f32[32,128]{1,0:T(8,128)}) custom-call(bf16[128,4096]{1,0:T(8,128)(2,1)S(1)} %get-tuple-element.12.refs_0_, bf16[128,4096]{1,0:T(8,128)(2,1)S(1)} %get-tuple-element.13.refs_1_, bf16[128,4096]{1,0:T(8,128)(2,1)S(1)} %get-tuple-element.14.refs_2_, ...), custom_call_target="tpu_custom_call" | custom-call | tf_op jit(solution)/shard_map/write_out/pallas_call | solution.py:396

commit v3 on v2

--- a/solution.py
+++ b/solution.py
@@ -14,25 +14,19 @@
 F = HEADS * HD
 HALF = HEADS // 2
 SIDE = 4
-CHIPS = SIDE * SIDE
+ROWS = HD // SIDE
 DP = 8
-GROUPS = (8, 8)
+GROUPS = (4, 4, 4, 4)
 G = len(GROUPS)
 FIRST = [sum(GROUPS[:g]) for g in range(G)]
+LEAD = 2
+GAIN_POINTS = ("F0", "F2", "F3", "E", "B2")
 MESH = pl.DeviceIdType.MESH
 F32 = jnp.float32
 BF16 = jnp.bfloat16
 
-OFFSETS = [(dy, dx) for dy in range(SIDE) for dx in range(SIDE) if (dy, dx) != (0, 0)]
-N_OFF = len(OFFSETS)
-
-
 def dot(a, b, ca, cb):
     return lax.dot_general(a, b, (((ca,), (cb,)), ((), ())), preferred_element_type=F32)
-
-
-def tiles(g, scan):
-    return GROUPS[g] + (1 if scan == 1 and g == G - 1 else 0)
 
 
 def scratch_shapes():
@@ -43,12 +37,14 @@
     shapes["load_sem"] = pltpu.SemaphoreType.DMA((5,))
     for s in range(2):
         for g in range(G):
-            n = tiles(g, s)
-            shapes[f"own{s}{g}"] = pltpu.VMEM((2, CHIPS, n, 8, HD), F32)
-            for name in ("pair", "sums", "gath", "give", "back", "hand", "taken"):
-                shapes[f"{name}{s}{g}"] = pltpu.VMEM((CHIPS, n, 8, HD), F32)
-        for name in ("out_s", "out_r", "back_s", "back_r", "pair_s", "pair_r", "hand_s", "hand_r"):
-            shapes[f"{name}{s}"] = pltpu.SemaphoreType.DMA((G,))
+            n = GROUPS[g]
+            shapes[f"own{s}{g}"] = pltpu.VMEM((2, SIDE, n, ROWS, HD), F32)
+            shapes[f"total{s}{g}"] = pltpu.VMEM((n, ROWS, HD), F32)
+            for name in ("pair", "sums", "gath", "rows", "give", "back", "hand", "taken"):
+                shapes[f"{name}{s}{g}"] = pltpu.VMEM((SIDE, n, ROWS, HD), F32)
+        for name in ("pair", "out", "rows", "back", "hand"):
+            shapes[f"{name}_s{s}"] = pltpu.SemaphoreType.DMA((G,))
+            shapes[f"{name}_r{s}"] = pltpu.SemaphoreType.DMA((G,))
     shapes["prefix"] = pltpu.VMEM((HEADS, HD, HD), BF16)
     shapes["masked"] = pltpu.VMEM((HEADS, TOK, TOK), BF16)
     shapes["qt"] = pltpu.VMEM((HEADS, HD, TOK), BF16)
@@ -57,13 +53,14 @@
     shapes["grad"] = pltpu.VMEM((TOK, F), BF16)
     shapes["gk_part"] = pltpu.VMEM((TOK, F), F32)
     shapes["gv_part"] = pltpu.VMEM((TOK, F), F32)
-    shapes["zrow"] = pltpu.VMEM((DP, 8, HD), F32)
-    shapes["ztile"] = pltpu.VMEM((8, HD), F32)
-    shapes["gtile"] = pltpu.VMEM((8, HD), F32)
-    shapes["gback"] = pltpu.VMEM((CHIPS, 8, HD), F32)
-    shapes["gtaken"] = pltpu.VMEM((CHIPS, 8, HD), F32)
-    for name in ("z_s", "z_r", "gb_s", "gb_r", "gp_s", "gp_r"):
-        shapes[name] = pltpu.SemaphoreType.DMA((1,))
+    shapes["gain_own"] = pltpu.VMEM((2, SIDE, ROWS, HD), F32)
+    for name in ("gain_pair", "gain_sums", "gain_x", "gain_y", "gain_back", "gain_taken"):
+        shapes[name] = pltpu.VMEM((SIDE, ROWS, HD), F32)
+    shapes["gain_z"] = pltpu.VMEM((DP, ROWS, HD), F32)
+    for name in ("gain_ysend", "gain_zsend", "gain_bsend"):
+        shapes[name] = pltpu.VMEM((ROWS, HD), F32)
+    shapes["gain_s"] = pltpu.SemaphoreType.DMA((6,))
+    shapes["gain_r"] = pltpu.SemaphoreType.DMA((6,))
     return shapes
 
 
@@ -87,13 +84,19 @@
     other = 1 - core
     y, x = chip // SIDE, chip % SIDE
 
-    partner = (z, chip * 2 + other)
-    near = [((y + dy_) % SIDE) * SIDE + (x + dx_) % SIDE for dy_, dx_ in OFFSETS]
-    targets = [(z, c * 2 + core) for c in near]
-    z_targets = [((z + d) % DP, s_at) for d in range(1, DP)]
+    def device(y_at, x_at, core_at):
+        return (z, (y_at * SIDE + x_at) * 2 + core_at)
+
+    partner = device(y, x, other)
+    turns = [2, 1 + 2 * core, 3 - 2 * core]
+    x_near = [(x + d) % SIDE for d in turns]
+    x_targets = [device(y, c, core) for c in x_near]
+    y_targets = [device((y + d) % SIDE, x, core) for d in turns]
+    z_targets = [((z + d) % DP, s_at) for d in (1, 7, 2, 6, 3, 5, 4)]
 
     barrier = pltpu.get_barrier_semaphore()
-    for t in [partner] + targets + z_targets:
+    greeted = [partner] + x_targets + y_targets + z_targets
+    for t in greeted:
         pl.semaphore_signal(barrier, inc=1, device_id=t, device_id_type=MESH)
 
     pending = []
@@ -132,13 +135,14 @@
 
         return lax.fori_loop(0, count // step, some, carry)
 
-    def tile3(value):
-        return value.reshape(CHIPS, 8, HD)
+    def sliced(value):
+        return value.reshape(SIDE, ROWS, HD)
+
+    def sems(name, scan, g):
+        return m[f"{name}_s{scan}"].at[g], m[f"{name}_r{scan}"].at[g]
 
     def pair_send(scan, g):
-        return to_partner(
-            m[f"own{scan}{g}"].at[other], m[f"pair{scan}{g}"], m[f"pair_s{scan}"].at[g], m[f"pair_r{scan}"].at[g]
-        )
+        return to_partner(m[f"own{scan}{g}"].at[other], m[f"pair{scan}{g}"], *sems("pair", scan, g))
 
     def out_send(scan, g):
         sums, gath = m[f"sums{scan}{g}"], m[f"gath{scan}{g}"]
@@ -147,54 +151,56 @@
             sums[c] = m[f"own{scan}{g}"][core, c] + m[f"pair{scan}{g}"][c]
             return carry
 
-        lax.fori_loop(0, CHIPS, add, 0)
-        gath[chip] = sums[chip]
+        lax.fori_loop(0, SIDE, add, 0)
+        gath[x] = sums[x]
         return fan(
-            lambda i: sums.at[near[i]],
-            gath.at[chip],
-            m[f"out_s{scan}"].at[g],
-            m[f"out_r{scan}"].at[g],
-            targets,
-            gath.at[pl.ds(0, N_OFF)],
+            lambda i: sums.at[x_near[i]], gath.at[x], *sems("out", scan, g), x_targets, gath.at[pl.ds(0, SIDE - 1)]
         )
 
+    def rows_send(scan, g):
+        gath, total, rows = m[f"gath{scan}{g}"], m[f"total{scan}{g}"], m[f"rows{scan}{g}"]
+
+        def one(j, carry):
+            value = (gath[0, j] + gath[1, j]) + (gath[2, j] + gath[3, j])
+            total[j] = value
+            rows[y, j] = value
+            return carry
+
+        lax.fori_loop(0, GROUPS[g], one, 0)
+        return fan(lambda i: total, rows.at[y], *sems("rows", scan, g), y_targets, rows.at[pl.ds(0, SIDE - 1)])
+
     def back_send(scan, g):
-        gath, give, back = m[f"gath{scan}{g}"], m[f"give{scan}{g}"], m[f"back{scan}{g}"]
-
-        def one(t, carry):
-            total = jnp.zeros((8, HD), F32)
-            for c in range(CHIPS) if scan == 0 else reversed(range(CHIPS)):
-                give[c, t] = total
-                total = total + gath[c, t]
+        gath, rows, give, back = (m[f"{name}{scan}{g}"] for name in ("gath", "rows", "give", "back"))
+
+        def one(j, carry):
+            value = jnp.zeros((ROWS, HD), F32)
+            for c in range(SIDE):
+                value = value + jnp.where(c < y if scan == 0 else c > y, rows[c, j], 0.0)
+            for c in range(SIDE) if scan == 0 else reversed(range(SIDE)):
+                give[c, j] = value
+                value = value + gath[c, j]
             return carry
 
         lax.fori_loop(0, GROUPS[g], one, 0)
-        back[chip, :GROUPS[g]] = give[chip, :GROUPS[g]]
-        heads = pl.ds(0, GROUPS[g])
+        back[x] = give[x]
         return fan(
-            lambda i: give.at[near[i], heads],
-            back.at[chip, heads],
-            m[f"back_s{scan}"].at[g],
-            m[f"back_r{scan}"].at[g],
-            targets,
-            back.at[pl.ds(0, N_OFF), heads],
+            lambda i: give.at[x_near[i]],
+            back.at[x],
+            *sems("back", scan, g),
+            x_targets,
+            back.at[pl.ds(0, SIDE - 1)],
         )
 
     def hand_send(scan, g):
-        hand = m[f"hand{scan}{g}"]
+        hand, back, own = (m[f"{name}{scan}{g}"] for name in ("hand", "back", "own"))
         with_own = jnp.where(core == (0 if scan == 0 else 1), 1.0, 0.0).astype(F32)
 
         def add(c, carry):
-            hand[c, :GROUPS[g]] = m[f"back{scan}{g}"][c, :GROUPS[g]] + m[f"own{scan}{g}"][core, c, :GROUPS[g]] * with_own
-            return carry
-
-        lax.fori_loop(0, CHIPS, add, 0)
-        return to_partner(
-            hand.at[:, pl.ds(0, GROUPS[g])],
-            m[f"taken{scan}{g}"].at[:, pl.ds(0, GROUPS[g])],
-            m[f"hand_s{scan}"].at[g],
-            m[f"hand_r{scan}"].at[g],
-        )
+            hand[c] = back[c] + own[core, c] * with_own
+            return carry
+
+        lax.fori_loop(0, SIDE, add, 0)
+        return to_partner(hand, m[f"taken{scan}{g}"], *sems("hand", scan, g))
 
     def carried(scan, g, j, mine):
         if mine:
@@ -204,10 +210,63 @@
             value = m[f"taken{scan}{g}"][:, j]
         return value.reshape(HD, HD).astype(BF16)
 
+    def exchange(scan, pairs, ready, fill):
+        outs, totals, backs = [], [], []
+        for g in range(LEAD):
+            ready(g)
+            pairs[g]()
+            outs.append(out_send(scan, g))
+        for g in range(G):
+            fill(g)
+            outs[g]()
+            totals.append(rows_send(scan, g))
+            if g + LEAD < G:
+                pairs[g + LEAD]()
+                outs.append(out_send(scan, g + LEAD))
+            if g >= 1:
+                totals[g - 1]()
+                backs.append(back_send(scan, g - 1))
+        totals[G - 1]()
+        backs.append(back_send(scan, G - 1))
+        return backs
+
+    gain_wait = []
+
+    def gain_step(at):
+        step_sems = (m["gain_s"].at[at], m["gain_r"].at[at])
+        if at:
+            gain_wait[at - 1]()
+        if at == 0:
+            wait = to_partner(m["gain_own"].at[other], m["gain_pair"], *step_sems)
+        elif at == 1:
+            sums, got = m["gain_sums"], m["gain_x"]
+            sums[...] = m["gain_own"][core] + m["gain_pair"][...]
+            got[x] = sums[x]
+            wait = fan(lambda i: sums.at[x_near[i]], got.at[x], *step_sems, x_targets, got.at[pl.ds(0, SIDE - 1)])
+        elif at == 2:
+            wait = gain_fan("gain_x", "gain_ysend", "gain_y", y, y_targets, step_sems)
+        elif at == 3:
+            wait = gain_fan("gain_y", "gain_zsend", "gain_z", z, z_targets, step_sems)
+        elif at == 4:
+            wait = gain_fan("gain_z", "gain_bsend", "gain_back", x, x_targets, step_sems)
+        else:
+            wait = to_partner(m["gain_back"], m["gain_taken"], *step_sems)
+        gain_wait.append(wait)
+
+    def gain_fan(src, send, dst, slot, to, step_sems):
+        value = jnp.sum(m[src][...], axis=0)
+        m[send][...] = value
+        m[dst][slot] = value
+        return fan(lambda i: m[send], m[dst].at[slot], *step_sems, to, m[dst].at[pl.ds(0, len(to))])
+
+    def gain_result(ref):
+        total = ref[...].reshape(HALF, 8, HD).sum(axis=1)
+        return total * (1.0 / math.sqrt(DP * 32 * TOK))
+
     def states(half, g):
         def body(head, j, carry):
             at = lanes(head)
-            m[f"own0{g}"][half, :, j] = tile3(dot(k[:, at], v[:, at], 0, 0))
+            m[f"own0{g}"][half, :, j] = sliced(dot(k[:, at], v[:, at], 0, 0))
             return carry
 
         each_head(half * HALF + FIRST[g], GROUPS[g], body)
@@ -217,14 +276,10 @@
     for g in range(G):
         states(other, g)
     states(core, 0)
-    pl.semaphore_wait(barrier, 1 + N_OFF + DP - 1)
+    pl.semaphore_wait(barrier, len(greeted))
     pairs = [pair_send(0, g) for g in range(G)]
     for g in range(1, G):
         states(core, g)
-    outs = []
-    for g in range(G):
-        pairs[g]()
-        outs.append(out_send(0, g))
     for load in loads[2:]:
         load.wait()
 
@@ -245,12 +300,19 @@
         m["qt"][head] = q[:, at].T
         return carry
 
-    backs = []
-    for g in range(G):
-        each_head(2 * FIRST[g], 2 * GROUPS[g], local_part)
-        outs[g]()
-        backs.append(back_send(0, g))
-    each_head(0, HEADS, later_part)
+    def part(body, g):
+        each_head(2 * FIRST[g], 2 * GROUPS[g], body)
+
+    def fill(g):
+        if g == 0:
+            part(local_part, 0)
+            part(local_part, 1)
+        elif g < G - 1:
+            part(local_part, g + 1)
+        else:
+            each_head(0, HEADS, later_part)
+
+    backs = exchange(0, pairs, lambda g: None, fill)
 
     def attn_part(half, g, mine, acc):
         def body(head, j, acc):
@@ -283,9 +345,10 @@
             normed = m["attn"][:, at] * scale
             grad = (scale * (m["dnorm"][:, at] - normed * inner)).astype(BF16)
             m["grad"][:, at] = grad
-            term = tile3(dy[:, at].astype(F32) * normed).sum(axis=0)
-            m[f"own1{G - 1}"][half, FIRST[g] + j, GROUPS[G - 1]] = term
-            m[f"own1{g}"][half, :, j] = tile3(dot(m["qt"][head], grad, 1, 0))
+            term = (dy[:, at].astype(F32) * normed).reshape(TOK // 8, 8, HD).sum(axis=0)
+            nth = FIRST[g] + j
+            m["gain_own"][half, nth // SIDE, pl.ds(pl.multiple_of(nth % SIDE * 8, 8), 8)] = term
+            m[f"own1{g}"][half, :, j] = sliced(dot(m["qt"][head], grad, 1, 0))
             return carry
 
         each_head(half * HALF + FIRST[g], GROUPS[g], body)
@@ -294,11 +357,7 @@
     for g in range(G):
         gstates(other, g)
         pairs.append(pair_send(1, g))
-    outs = []
-    for g in range(G):
-        gstates(core, g)
-        pairs[g]()
-        outs.append(out_send(1, g))
+    gain_step(0)
 
     def grads_part(head, j, carry):
         at = lanes(head)
@@ -313,22 +372,28 @@
         m["gv_part"][:, at] = dot(m["masked"][head], m["grad"][:, at], 0, 0)
         return carry
 
-    backs = []
-    for g in range(G):
-        each_head(2 * FIRST[g], 2 * GROUPS[g], grads_part)
-        outs[g]()
-        if g == G - 1:
-            gath = m[f"gath1{g}"]
-            total = gath[0, GROUPS[g]]
-            for c in range(1, CHIPS):
-                total = total + gath[c, GROUPS[g]]
-            m["ztile"][...] = total
-            m["zrow"][z] = total
-            zs = fan(
-                lambda i: m["ztile"], m["zrow"].at[z], m["z_s"].at[0], m["z_r"].at[0], z_targets, m["zrow"].at[pl.ds(0, DP - 1)]
-            )
-        backs.append(back_send(1, g))
-    each_head(0, HEADS, value_part)
+    gain_steps = iter(range(1, 6))
+
+    def gain_at(point):
+        for _ in range(GAIN_POINTS.count(point)):
+            gain_step(next(gain_steps))
+
+    def fill(g):
+        if g == 0:
+            for later in range(LEAD, G):
+                gstates(core, later)
+        gain_at(f"F{g}")
+        if g == 0:
+            part(grads_part, 0)
+            part(grads_part, 1)
+        elif g < G - 1:
+            part(grads_part, g + 1)
+        else:
+            each_head(0, HEADS, value_part)
+
+    backs = exchange(1, pairs, lambda g: gstates(core, g), fill)
+
+    gain_at("E")
 
     def finish(half, g, mine):
         def body(head, j, carry):
@@ -341,29 +406,15 @@
         each_head(half * HALF + FIRST[g], GROUPS[g], body)
 
     for g in range(G):
-        if g == G - 1:
-            zs()
-            total = m["zrow"][0]
-            for i in range(1, DP):
-                total = total + m["zrow"][i]
-            total = jnp.sum(total, axis=0, keepdims=True) * (1.0 / math.sqrt(DP * 32 * TOK))
-            total = jnp.broadcast_to(total, (8, HD))
-            m["gtile"][...] = total
-            m["gback"][chip] = total
-            gbs = fan(
-                lambda i: m["gtile"], m["gback"].at[chip], m["gb_s"].at[0], m["gb_r"].at[0], targets, m["gback"].at[pl.ds(0, N_OFF)]
-            )
         backs[g]()
         hand = hand_send(1, g)
+        gain_at(f"B{g}")
         finish(core, g, True)
-        if g == G - 1:
-            gbs()
-            gp = to_partner(m["gback"], m["gtaken"], m["gp_s"].at[0], m["gp_r"].at[0])
         hand()
         finish(other, g, False)
-    gg_ref[pl.ds(core * HALF, HALF)] = m["gback"][:, 0, :]
-    gp()
-    gg_ref[pl.ds(other * HALF, HALF)] = m["gtaken"][:, 0, :]
+    gg_ref[pl.ds(pl.multiple_of(core * HALF, HALF), HALF)] = gain_result(m["gain_back"])
+    gain_wait[5]()
+    gg_ref[pl.ds(pl.multiple_of(other * HALF, HALF), HALF)] = gain_result(m["gain_taken"])
     for wait in pending:
         wait()
 

time: 75.4 us -> 73.4 us (0.973)
  Pallas kernels: 74.7 us -> 72.7 us
    pallas_call x1, Pallas kernels: 73 us -> 71 us  [shards(): pl.pallas_call(kernel, out_shape=kept, in_specs=[hbm] * 5, out_specs=(vme...]
where the time goes in v3:
time: 73.4 us
  Pallas kernels  72.7 us (99%)
    pallas_call x1, Pallas kernels, shards(): pl.pallas_call(kernel, out_shape=kept, in_specs=[hbm] * 5, out_specs=(vme...  71 us
    pallas_call x1, Pallas kernels, shards(): pl.pallas_call(write_out, out_shape=tuple((jax.ShapeDtypeStruct(r.shape,...  1.7 us

profile of v3, /device:TPU:1, one launch (start us, length us, event | category | flops | bytes accessed | tf_op | source)
XLA Modules:
  0.0 73.4 jit_solution(9109916255380682214)
XLA Ops:
  0.6 71.0 %scan_grads.1 = (bf16[128,4096]{1,0:T(8,128)(2,1)S(1)}, bf16[128,4096]{1,0:T(8,128)(2,1)S(1)}, bf16[128,4096]{1,0:T(8,128)(2,1)S(1)}, f32[32,128]{1,0:T(8,128)S(1)}) custom-call(bf16[128,4096]{1,0:T(8,128)(2,1)} %bitcast.9, bf16[128,4096]{1,0:T(8,128)(2,1)} %bitcast.10, bf16[128,4096]{1,0:T(8,128)(2,1)} %bitcast.11, bf16[128,4096]{1,0:T(8,128)(2,1)} %bitcast.12, ...), custom_call_target="tpu_custom_call" | custom-call | tf_op jit(solution)/shard_map/scan_grads/pallas_call | solution.py:436
  71.7 1.7 %write_out.1 = (bf16[128,4096]{1,0:T(8,128)(2,1)}, bf16[128,4096]{1,0:T(8,128)(2,1)}, bf16[128,4096]{1,0:T(8,128)(2,1)}, f32[32,128]{1,0:T(8,128)}) custom-call(bf16[128,4096]{1,0:T(8,128)(2,1)S(1)} %get-tuple-element.12.refs_0_, bf16[128,4096]{1,0:T(8,128)(2,1)S(1)} %get-tuple-element.13.refs_1_, bf16[128,4096]{1,0:T(8,128)(2,1)S(1)} %get-tuple-element.14.refs_2_, ...), custom_call_target="tpu_custom_call" | custom-call | tf_op jit(solution)/shard_map/write_out/pallas_call | solution.py:447

commit v4 on v3

--- a/solution.py
+++ b/solution.py
@@ -16,11 +16,11 @@
 SIDE = 4
 ROWS = HD // SIDE
 DP = 8
-GROUPS = (4, 4, 4, 4)
+GROUPS = (2, 4, 4, 4, 2)
 G = len(GROUPS)
 FIRST = [sum(GROUPS[:g]) for g in range(G)]
 LEAD = 2
-GAIN_POINTS = ("F0", "F2", "F3", "E", "B2")
+GAIN_POINTS = ("F0", "F3", "F4", "E", "B3")
 MESH = pl.DeviceIdType.MESH
 F32 = jnp.float32
 BF16 = jnp.bfloat16
@@ -42,9 +42,11 @@
             shapes[f"total{s}{g}"] = pltpu.VMEM((n, ROWS, HD), F32)
             for name in ("pair", "sums", "gath", "rows", "give", "back", "hand", "taken"):
                 shapes[f"{name}{s}{g}"] = pltpu.VMEM((SIDE, n, ROWS, HD), F32)
-        for name in ("pair", "out", "rows", "back", "hand"):
+        for name in ("pair", "out", "back", "hand"):
             shapes[f"{name}_s{s}"] = pltpu.SemaphoreType.DMA((G,))
             shapes[f"{name}_r{s}"] = pltpu.SemaphoreType.DMA((G,))
+        shapes[f"rows_s{s}"] = pltpu.SemaphoreType.DMA((G, SIDE - 1))
+        shapes[f"rows_r{s}"] = pltpu.SemaphoreType.DMA((G, SIDE - 1))
     shapes["prefix"] = pltpu.VMEM((HEADS, HD, HD), BF16)
     shapes["masked"] = pltpu.VMEM((HEADS, TOK, TOK), BF16)
     shapes["qt"] = pltpu.VMEM((HEADS, HD, TOK), BF16)
@@ -74,8 +76,6 @@
         pltpu.make_async_copy(src, dst, m["load_sem"].at[i])
         for i, (src, dst) in enumerate(((k_hbm, k), (v_hbm, v), (q_hbm, q), (dy_hbm, dy), (gain_hbm, gain)))
     ]
-    for load in loads:
-        load.start()
 
     z = lax.axis_index("dp")
     s_at = lax.axis_index("seq")
@@ -98,6 +98,8 @@
     greeted = [partner] + x_targets + y_targets + z_targets
     for t in greeted:
         pl.semaphore_signal(barrier, inc=1, device_id=t, device_id_type=MESH)
+    for load in loads:
+        load.start()
 
     pending = []
 
@@ -167,7 +169,28 @@
             return carry
 
         lax.fori_loop(0, GROUPS[g], one, 0)
-        return fan(lambda i: total, rows.at[y], *sems("rows", scan, g), y_targets, rows.at[pl.ds(0, SIDE - 1)])
+        sign = 1 if scan == 0 else -1
+
+        def in_side(at):
+            return (at >= 0) & (at < SIDE)
+
+        def copy(d):
+            return pltpu.make_async_remote_copy(
+                src_ref=total,
+                dst_ref=rows.at[y],
+                send_sem=m[f"rows_s{scan}"].at[g, d - 1],
+                recv_sem=m[f"rows_r{scan}"].at[g, d - 1],
+                device_id=device((y + sign * d + SIDE) % SIDE, x, core),
+                device_id_type=MESH,
+            )
+
+        def each(active, act):
+            for d in range(1, SIDE):
+                pl.when(active(d))(lambda d=d: act(d))
+
+        each(lambda d: in_side(y + sign * d), lambda d: copy(d).start())
+        pending.append(lambda: each(lambda d: in_side(y + sign * d), lambda d: copy(d).wait_send()))
+        return lambda: each(lambda d: in_side(y - sign * d), lambda d: copy(d).wait_recv())
 
     def back_send(scan, g):
         gath, rows, give, back = (m[f"{name}{scan}{g}"] for name in ("gath", "rows", "give", "back"))
@@ -210,12 +233,23 @@
             value = m[f"taken{scan}{g}"][:, j]
         return value.reshape(HD, HD).astype(BF16)
 
-    def exchange(scan, pairs, ready, fill):
-        outs, totals, backs = [], [], []
+    def exchange(scan, make, fill):
+        pairs, outs, totals, backs = [], [], [], []
+
+        def pair(g):
+            make(other, g)
+            pairs.append(pair_send(scan, g))
+
         for g in range(LEAD):
-            ready(g)
+            pair(g)
+        for g in range(LEAD):
+            make(core, g)
             pairs[g]()
             outs.append(out_send(scan, g))
+            if LEAD + g < G:
+                pair(LEAD + g)
+        for g in range(2 * LEAD, G):
+            pair(g)
         for g in range(G):
             fill(g)
             outs[g]()
@@ -229,6 +263,11 @@
         totals[G - 1]()
         backs.append(back_send(scan, G - 1))
         return backs
+
+    def drain():
+        for wait in pending:
+            wait()
+        pending.clear()
 
     gain_wait = []
 
@@ -275,13 +314,8 @@
     loads[1].wait()
     for g in range(G):
         states(other, g)
-    states(core, 0)
+        states(core, g)
     pl.semaphore_wait(barrier, len(greeted))
-    pairs = [pair_send(0, g) for g in range(G)]
-    for g in range(1, G):
-        states(core, g)
-    for load in loads[2:]:
-        load.wait()
 
     rows = lax.broadcasted_iota(jnp.int32, (TOK, TOK), 0)
     cols = lax.broadcasted_iota(jnp.int32, (TOK, TOK), 1)
@@ -305,6 +339,8 @@
 
     def fill(g):
         if g == 0:
+            for load in loads[2:]:
+                load.wait()
             part(local_part, 0)
             part(local_part, 1)
         elif g < G - 1:
@@ -312,7 +348,7 @@
         else:
             each_head(0, HEADS, later_part)
 
-    backs = exchange(0, pairs, lambda g: None, fill)
+    backs = exchange(0, lambda half, g: None, fill)
 
     def attn_part(half, g, mine, acc):
         def body(head, j, acc):
@@ -327,11 +363,13 @@
         return each_head(half * HALF + FIRST[g], GROUPS[g], body, acc)
 
     acc = (jnp.zeros((TOK, HD), F32), jnp.zeros((TOK, HD), F32))
+    hands = []
     for g in range(G):
         backs[g]()
-        hand = hand_send(0, g)
+        hands.append(hand_send(0, g))
         acc = attn_part(core, g, True, acc)
-        hand()
+    for g in range(G):
+        hands[g]()
         acc = attn_part(other, g, False, acc)
     sq, cross = acc
     scale = lax.rsqrt(jnp.sum(sq, axis=1, keepdims=True) * (1.0 / F) + 1e-06)
@@ -353,12 +391,6 @@
 
         each_head(half * HALF + FIRST[g], GROUPS[g], body)
 
-    pairs = []
-    for g in range(G):
-        gstates(other, g)
-        pairs.append(pair_send(1, g))
-    gain_step(0)
-
     def grads_part(head, j, carry):
         at = lanes(head)
         g_h = m["grad"][:, at]
@@ -380,6 +412,7 @@
 
     def fill(g):
         if g == 0:
+            gain_step(0)
             for later in range(LEAD, G):
                 gstates(core, later)
         gain_at(f"F{g}")
@@ -391,7 +424,7 @@
         else:
             each_head(0, HEADS, value_part)
 
-    backs = exchange(1, pairs, lambda g: gstates(core, g), fill)
+    backs = exchange(1, gstates, fill)
 
     gain_at("E")
 
@@ -405,18 +438,20 @@
 
         each_head(half * HALF + FIRST[g], GROUPS[g], body)
 
+    drain()
+    hands = []
     for g in range(G):
         backs[g]()
-        hand = hand_send(1, g)
+        hands.append(hand_send(1, g))
         gain_at(f"B{g}")
         finish(core, g, True)
-        hand()
+    for g in range(G):
+        hands[g]()
         finish(other, g, False)
     gg_ref[pl.ds(pl.multiple_of(core * HALF, HALF), HALF)] = gain_result(m["gain_back"])
     gain_wait[5]()
     gg_ref[pl.ds(pl.multiple_of(other * HALF, HALF), HALF)] = gain_result(m["gain_taken"])
-    for wait in pending:
-        wait()
+    drain()
 
 
 def write_out(*refs):

time: 73.4 us -> 72.3 us (0.985)
  Pallas kernels: 72.7 us -> 71.6 us
    pallas_call x1, Pallas kernels: 71 us -> 69.9 us  [shards(): pl.pallas_call(kernel, out_shape=kept, in_specs=[hbm] * 5, out_specs=(vme...]
where the time goes in v4:
time: 72.3 us
  Pallas kernels  71.6 us (99%)
    pallas_call x1, Pallas kernels, shards(): pl.pallas_call(kernel, out_shape=kept, in_specs=[hbm] * 5, out_specs=(vme...  69.9 us
    pallas_call x1, Pallas kernels, shards(): pl.pallas_call(write_out, out_shape=tuple((jax.ShapeDtypeStruct(r.shape,...  1.7 us

profile of v4, /device:TPU:1, one launch (start us, length us, event | category | flops | bytes accessed | tf_op | source)
XLA Modules:
  0.0 72.3 jit_solution(9478523306686839757)
XLA Ops:
  0.6 69.9 %scan_grads.1 = (bf16[128,4096]{1,0:T(8,128)(2,1)S(1)}, bf16[128,4096]{1,0:T(8,128)(2,1)S(1)}, bf16[128,4096]{1,0:T(8,128)(2,1)S(1)}, f32[32,128]{1,0:T(8,128)S(1)}) custom-call(bf16[128,4096]{1,0:T(8,128)(2,1)} %bitcast.9, bf16[128,4096]{1,0:T(8,128)(2,1)} %bitcast.10, bf16[128,4096]{1,0:T(8,128)(2,1)} %bitcast.11, bf16[128,4096]{1,0:T(8,128)(2,1)} %bitcast.12, ...), custom_call_target="tpu_custom_call" | custom-call | tf_op jit(solution)/shard_map/scan_grads/pallas_call | solution.py:471
  70.6 1.7 %write_out.1 = (bf16[128,4096]{1,0:T(8,128)(2,1)}, bf16[128,4096]{1,0:T(8,128)(2,1)}, bf16[128,4096]{1,0:T(8,128)(2,1)}, f32[32,128]{1,0:T(8,128)}) custom-call(bf16[128,4096]{1,0:T(8,128)(2,1)S(1)} %get-tuple-element.12.refs_0_, bf16[128,4096]{1,0:T(8,128)(2,1)S(1)} %get-tuple-element.13.refs_1_, bf16[128,4096]{1,0:T(8,128)(2,1)S(1)} %get-tuple-element.14.refs_2_, ...), custom_call_target="tpu_custom_call" | custom-call | tf_op jit(solution)/shard_map/write_out/pallas_call | solution.py:482

commit v5 on v4

--- a/solution.py
+++ b/solution.py
@@ -16,11 +16,11 @@
 SIDE = 4
 ROWS = HD // SIDE
 DP = 8
-GROUPS = (2, 4, 4, 4, 2)
+GROUPS = (2, 2, 4, 4, 2, 2)
 G = len(GROUPS)
 FIRST = [sum(GROUPS[:g]) for g in range(G)]
-LEAD = 2
-GAIN_POINTS = ("F0", "F3", "F4", "E", "B3")
+LEAD = 3
+GAIN_POINTS = ("F0", "F3", "F5", "E", "B4")
 MESH = pl.DeviceIdType.MESH
 F32 = jnp.float32
 BF16 = jnp.bfloat16

time: 72.3 us -> 72.7 us (level)
  no operation moved by 1% of the time
where the time goes in v5:
time: 72.7 us; the launch traced here: 72.6 us
  Pallas kernels  72 us (99%)
    pallas_call x1, Pallas kernels, shards(): pl.pallas_call(kernel, out_shape=kept, in_specs=[hbm] * 5, out_specs=(vme...  70.3 us
    pallas_call x1, Pallas kernels, shards(): pl.pallas_call(write_out, out_shape=tuple((jax.ShapeDtypeStruct(r.shape,...  1.7 us

profile of v5, /device:TPU:1, one launch (start us, length us, event | category | flops | bytes accessed | tf_op | source)
XLA Modules:
  0.0 72.6 jit_solution(2178183967013728789)
XLA Ops:
  0.6 70.3 %scan_grads.1 = (bf16[128,4096]{1,0:T(8,128)(2,1)S(1)}, bf16[128,4096]{1,0:T(8,128)(2,1)S(1)}, bf16[128,4096]{1,0:T(8,128)(2,1)S(1)}, f32[32,128]{1,0:T(8,128)S(1)}) custom-call(bf16[128,4096]{1,0:T(8,128)(2,1)} %bitcast.9, bf16[128,4096]{1,0:T(8,128)(2,1)} %bitcast.10, bf16[128,4096]{1,0:T(8,128)(2,1)} %bitcast.11, bf16[128,4096]{1,0:T(8,128)(2,1)} %bitcast.12, ...), custom_call_target="tpu_custom_call" | custom-call | tf_op jit(solution)/shard_map/scan_grads/pallas_call | solution.py:471
  70.9 1.7 %write_out.1 = (bf16[128,4096]{1,0:T(8,128)(2,1)}, bf16[128,4096]{1,0:T(8,128)(2,1)}, bf16[128,4096]{1,0:T(8,128)(2,1)}, f32[32,128]{1,0:T(8,128)}) custom-call(bf16[128,4096]{1,0:T(8,128)(2,1)S(1)} %get-tuple-element.12.refs_0_, bf16[128,4096]{1,0:T(8,128)(2,1)S(1)} %get-tuple-element.13.refs_1_, bf16[128,4096]{1,0:T(8,128)(2,1)S(1)} %get-tuple-element.14.refs_2_, ...), custom_call_target="tpu_custom_call" | custom-call | tf_op jit(solution)/shard_map/write_out/pallas_call | solution.py:482
